TPU v7x, 1024 devices: a whole 4x8x16 slice. The times are simulated.
1024 devices in a mesh: pipe: 8 (over z_lo), seq: 16 (over y, z_hi), exp: 8 (over x, core).
Axes of the slice: x: 4, y: 8, z: 16 (z_hi: 2, z_lo: 8; z = z_hi * 8 + z_lo), core: 2. Of those that a mesh axis runs over, the one named last changes fastest.
Arguments:
- queries: bfloat16 [8, 8, 2048, 4096], P('pipe', 'exp', 'seq'), may hold values from -160 to 160
- key_rows: bfloat16 [8, 8, 2048, 256], P('pipe', 'exp', 'seq'), may hold values from -160 to 160
- value_rows: bfloat16 [8, 8, 2048, 256], P('pipe', 'exp', 'seq'), may hold values from -6 to 6
- residual: bfloat16 [8, 8, 2048, 4096], P('pipe', 'exp', 'seq'), may hold values from -6 to 6
- doc_lengths: int32 [8, 8, 8], P('pipe', 'exp'), may hold values from 1 to 512, 2048 in all within a row
- norm_gain: float32 [8, 4096], P('pipe'), may hold values from 0.1 to 1.9
- kv_weight: bfloat16 [8, 4096, 512], P('pipe', ('seq', 'exp')), may hold values from -0.09375 to 0.09375
Outputs:
- context: bfloat16 [8, 8, 2048, 4096], P('pipe', 'exp', 'seq')
- kv_next: bfloat16 [8, 8, 2048, 512], P('pipe', 'exp', 'seq')
Inputs may be any that keep to these rules, and one draw needn't show every extreme that they name: `doc_lengths`: every pack has a document of exactly 512 tokens and none longer.
All inputs are finite; a program needn't handle non-finite values.
Results may differ from a plain program's by a relative error of at most 0.0058.
Values may be sent and summed in bfloat16 or wider, within the bound.
A program may use at most 64 MiB of HBM per device.

v0:
```python
import math

import jax
import jax.numpy as jnp
from jax import lax
from jax.sharding import Mesh
from jax.sharding import PartitionSpec as P

DH = 128
SEQ = ("seq_0", "seq_1")
SEQ_EXP = ("seq_0", "seq_1", "exp")


epsilon = 1e-06


def gather_axes(shard, axes, dim):
    for axis in reversed(axes):
        shard = lax.all_gather(shard, axis, axis=dim, tiled=True)
    return shard


def shifted(block, axis, distance):
    devices = range(lax.axis_size(axis))
    route = [(i - distance, i) for i in devices if i - distance in devices]
    return lax.ppermute(block, axis, route)


def to_natural(rows, groups, tok_rows):
    half_rows = tok_rows // 2
    shaped = rows.reshape(groups, 2, half_rows, rows.shape[-1])
    first_half = shaped[:, 0].reshape(groups * half_rows, rows.shape[-1])
    second = shaped[::-1, 1].reshape(groups * half_rows, rows.shape[-1])
    return jnp.concatenate([first_half, second], axis=0)


def attend_run(
    query_run, first_pos, key_nat, value_nat, doc_ids, window, seq_rows, kv_heads, score_scale
):
    half_rows = query_run.shape[0]
    start = jnp.clip(first_pos + half_rows - window, 0, seq_rows - window)
    key_win = lax.dynamic_slice_in_dim(key_nat, start, window, 0)
    value_win = lax.dynamic_slice_in_dim(value_nat, start, window, 0)
    doc_win = lax.dynamic_slice_in_dim(doc_ids, start, window, 0)
    doc_query = lax.dynamic_slice_in_dim(doc_ids, first_pos, half_rows, 0)
    key_pos = start + jnp.arange(window, dtype=jnp.int32)
    query_pos = first_pos + jnp.arange(half_rows, dtype=jnp.int32)
    visible = (doc_query[:, None] == doc_win[None, :]) & (key_pos[None, :] <= query_pos[:, None])
    query_heads = query_run.reshape(half_rows, kv_heads, -1, DH)
    scores = (
        jnp.einsum("qgjd,kgd->qgjk", query_heads, key_win, preferred_element_type=jnp.float32)
        * score_scale
    )
    masked = jnp.where(visible[:, None, None, :], scores, -1e30)
    row_max = jnp.max(masked, axis=3, keepdims=True)
    weights = jnp.exp(masked - row_max)
    sums = jnp.sum(weights, axis=3, keepdims=True)
    rounded = weights.astype(jnp.bfloat16)
    mixed_rows = (
        jnp.einsum("qgjk,kgd->qgjd", rounded, value_win, preferred_element_type=jnp.float32) / sums
    )
    return mixed_rows.astype(jnp.bfloat16).reshape(half_rows, -1)


def on_device(queries, key_rows, value_rows, residual, doc_lengths, norm_gain, kv_weight):
    tok_rows = queries.shape[2]
    row_width = queries.shape[3]
    groups = lax.axis_size(SEQ)
    kv_heads = key_rows.shape[3] // DH
    seq_rows = tok_rows * groups
    longest = seq_rows // 4
    score_scale = 1.0 / math.sqrt(DH)
    key_local = key_rows.reshape(tok_rows, kv_heads, 1, DH)
    value_local = value_rows.reshape(tok_rows, kv_heads, 1, DH)
    pair_local = jnp.concatenate([key_local, value_local], axis=2).reshape(
        tok_rows, kv_heads, 2 * DH
    )
    bounds = jnp.cumsum(doc_lengths.reshape(-1))
    positions = jnp.arange(seq_rows, dtype=jnp.int32)
    doc_ids = jnp.sum((positions[:, None] >= bounds[None, :]).astype(jnp.int32), axis=1)
    full_weight = lax.all_gather(kv_weight, SEQ_EXP, axis=1, tiled=True)
    pair_every = gather_axes(pair_local.reshape(tok_rows, kv_heads * 2 * DH), SEQ, 0)
    pair_nat = to_natural(pair_every, groups, tok_rows).reshape(seq_rows, kv_heads, 2 * DH)
    key_nat = pair_nat[:, :, :DH]
    value_nat = pair_nat[:, :, DH:]
    half_rows = tok_rows // 2
    window = longest + half_rows
    own = lax.axis_index(SEQ)
    query_rows = queries.reshape(tok_rows, row_width)
    first_run = attend_run(
        query_rows[:half_rows],
        own * half_rows,
        key_nat,
        value_nat,
        doc_ids,
        window,
        seq_rows,
        kv_heads,
        score_scale,
    )
    second_run = attend_run(
        query_rows[half_rows:],
        (2 * groups - 1 - own) * half_rows,
        key_nat,
        value_nat,
        doc_ids,
        window,
        seq_rows,
        kv_heads,
        score_scale,
    )
    context_local = jnp.concatenate([first_run, second_run], axis=0)
    layer_out = (
        residual.reshape(tok_rows, row_width).astype(jnp.float32)
        + context_local.astype(jnp.float32)
    ).astype(jnp.bfloat16)
    received = shifted(layer_out, "pipe", 1)
    as_float = received.astype(jnp.float32)
    mean_square = jnp.mean(as_float * as_float, axis=1, keepdims=True)
    normed = (as_float * lax.rsqrt(mean_square + epsilon) * norm_gain).astype(jnp.bfloat16)
    projected = jnp.dot(
        normed,
        full_weight.reshape(row_width, kv_weight.shape[2]),
        preferred_element_type=jnp.float32,
    )
    kv_next = projected.astype(jnp.bfloat16)
    return (
        context_local.reshape(1, 1, tok_rows, row_width),
        kv_next.reshape(1, 1, tok_rows, kv_weight.shape[2]),
    )


def solution(mesh):
    finer = Mesh(
        mesh.devices.reshape(mesh.shape["pipe"], 8, 2, mesh.shape["exp"]),
        ("pipe", "seq_0", "seq_1", "exp"),
    )
    placed = (
        P("pipe", "exp", SEQ, None),
        P("pipe", "exp", SEQ, None),
        P("pipe", "exp", SEQ, None),
        P("pipe", "exp", SEQ, None),
        P("pipe", "exp", None),
        P("pipe", None),
        P("pipe", SEQ_EXP, None),
    )
    return jax.shard_map(
        on_device,
        mesh=finer,
        in_specs=placed,
        out_specs=(P("pipe", "exp", SEQ, None), P("pipe", "exp", SEQ, None)),
        check_vma=False,
    )
```

profile of v0, /device:TPU:1, one launch (start us, length us, event | category | flops | bytes accessed | tf_op | source)
XLA Modules:
  0.0 292.7 jit_solution(15722322288828809674)
XLA Ops:
  7.2 0.9 copy.28
  8.2 1.0 copy.29
  9.2 26.2 %all_gather.9 = bf16[256,512]{0,1:T(8,128)(2,1)} all-gather(bf16[128,512]{0,1:T(8,128)(2,1)S(1)} %bitcast.108), channel_id=1, replica_groups=mesh['pipe'=8,'seq_0'=8,'seq_1'=2,'exp'=8] {'seq_1'}, dimensions={0}, use_global_device_ids=true | all-gather | bytes 393216 | tf_op jit(solution)/shard_map/all_gather | solution.py:19
  35.5 0.7 all-gather.5.cloned.1.call-update
  36.2 0.8 reduce-window.8
  37.1 1.3 slice_bitcast_fusion
  38.9 0.1 compare_and_fusion.1
  39.0 53.2 %all-gather.3.cloned.1.call-done = bf16[2048,512]{0,1:T(8,128)(2,1)} async-done(((bf16[256,512]{0,1:T(8,128)(2,1)}), bf16[2048,512]{0,1:T(8,128)(2,1)}) %all-gather.3.cloned.1.call-update) | async-done | bytes 2097168 | tf_op jit(solution)/shard_map/all_gather | solution.py:19
  92.2 2.9 copy.30
  95.0 1.5 fusion.58
  96.5 1.3 concatenate.15
  97.9 2.3 rev.3
  100.1 1.3 concatenate.16
  101.5 0.1 copy_dynamic-update-slice_fusion.1
  101.6 0.1 copy_dynamic-update-slice_fusion
  101.8 0.4 fusion.57
  102.2 1.4 fusion.7
  103.6 1.4 fusion.2
  105.0 1.7 divide_convert_fusion
  106.8 0.3 copy.36
  107.1 1.4 fusion.6
  108.6 1.4 fusion
  110.0 1.7 divide_convert_fusion.1
  111.8 0.3 copy.34
  112.1 0.2 bitcast_dynamic-update-slice_fusion.1
  112.3 0.2 bitcast_dynamic-update-slice_fusion
  112.5 0.2 fusion.17
  112.7 3.2 %collective-permute-start = (bf16[128,4096]{1,0:T(8,128)(2,1)S(1)}, bf16[128,4096]{1,0:T(8,128)(2,1)S(1)}, u32[]{:S(2)}, u32[]{:S(2)}) collective-permute-start(bf16[128,4096]{1,0:T(8,128)(2,1)S(1)} %fusion.17), channel_id=1, source_target_pairs={{0,128},{128,256},{256,384},{384,512},{512,640},{640,768},{768,896... | collective-permute-start | bytes 3145736 | tf_op jit(solution)/shard_map/ppermute | solution.py:26
  116.0 18.6 %collective-permute-done = bf16[128,4096]{1,0:T(8,128)(2,1)S(1)} collective-permute-done((bf16[128,4096]{1,0:T(8,128)(2,1)S(1)}, bf16[128,4096]{1,0:T(8,128)(2,1)S(1)}, u32[]{:S(2)}, u32[]{:S(2)}) %collective-permute-start) | collective-permute-done | bytes 1048608 | tf_op jit(solution)/shard_map/ppermute | solution.py:26
  134.6 0.3 fusion.14
  134.9 147.3 %all-gather.5.cloned.1.call-done = bf16[1,4096,512]{2,1,0:T(8,128)(2,1)} async-done(((bf16[1,32,512]{2,1,0:T(8,128)(2,1)}), bf16[1,4096,512]{2,1,0:T(8,128)(2,1)}) %all-gather.5.cloned.1.call-update) | async-done | bytes 4194320 | tf_op jit(solution)/shard_map/all_gather | solution.py:81
  282.2 3.6 %fusion.27 = bf16[1,1,128,512]{3,2,1,0:T(8,128)(2,1)} fusion(bf16[1,4096,512]{2,1,0:T(8,128)(2,1)} %all-gather.5.cloned.1.call-done, bf16[128,4096]{1,0:T(8,128)(2,1)S(1)} %collective-permute-done, f32[4096]{0:T(1024)S(1)} %bitcast.112, f32[128]{0:T(128)S(1)} %add_rsqrt_fusion), kind=kOutput, calls=%fused_computation.26 | convolution fusion | flops 539033600 | bytes 5390848 | tf_op jit(solution)/shard_map/dot_general | solution.py:121
  (19 shorter events, 0.7 us)
Async XLA Ops:
  7.2 85.0 %all-gather.3.cloned.1.call-start = ((), (), s32[]{:S(2)}) async-start(), calls=%async_computation | async-start | bytes 2359296 | tf_op jit(solution)/shard_map/all_gather | solution.py:19
  35.4 246.8 %all-gather.5.cloned.1.call-start = ((), (), s32[]{:S(2)}) async-start(), calls=%async_computation.1 | async-start | bytes 4227072 | tf_op jit(solution)/shard_map/all_gather | solution.py:81
  110.0 2.5 copy-start.1
  111.7 170.5 %copy-start.2 = (f32[1,4096]{1,0:T(1,128)S(1)}, f32[1,4096]{1,0:T(1,128)}, u32[]{:S(2)}) copy-start(f32[1,4096]{1,0:T(1,128)} %param.12) | copy-start | bytes 49156
  112.5 173.3 %copy-start = (bf16[128,4096]{1,0:T(8,128)(2,1)}, bf16[128,4096]{1,0:T(8,128)(2,1)S(1)}, u32[]{:S(2)}) copy-start(bf16[128,4096]{1,0:T(8,128)(2,1)S(1)} %bitcast_dynamic-update-slice_fusion) | copy-start | bytes 3145732
  112.7 21.9 %collective-permute-start = (bf16[128,4096]{1,0:T(8,128)(2,1)S(1)}, bf16[128,4096]{1,0:T(8,128)(2,1)S(1)}, u32[]{:S(2)}, u32[]{:S(2)}) collective-permute-start(bf16[128,4096]{1,0:T(8,128)(2,1)S(1)} %fusion.17), channel_id=1, source_target_pairs={{0,128},{128,256},{256,384},{384,512},{512,640},{640,768},{768,896... | collective-permute-start | bytes 3145736 | tf_op jit(solution)/shard_map/ppermute | solution.py:26
Sparse Core Ops, SparseCore 0:
  35.5 56.5 all-gather.2
  98.0 184.2 all-gather.4
where the time goes:
time: 293 us
  waiting for transfers between devices  220 us (75%)
  blocking collectives  26.2 us (9%)
  local copies, waits for them, and re-layouts  14.4 us (5%)
  between operations  14.3 us (5%)
  matrix products  9.89 us (3%)
  other arithmetic  4.74 us (2%)
  starting transfers between devices  3.3 us (1%)
    all_gather x1, waiting for transfers between devices, on_device(): full_weight = lax.all_gather(kv_weight, SEQ_EXP, axis=1, tiled=True)  147 us
    all_gather x1, waiting for transfers between devices, gather_axes(): shard = lax.all_gather(shard, axis, axis=dim, tiled=True)  53.2 us
    all_gather x1, blocking collectives, gather_axes(): shard = lax.all_gather(shard, axis, axis=dim, tiled=True)  26.2 us
    ppermute x1, waiting for transfers between devices, shifted(): return lax.ppermute(block, axis, route)  18.6 us
  transfers between devices with their start and end apart: 3, of which 3 were waited for; matrix products, arithmetic and copies ran while one was open for 8% of the time, Pallas kernels for 0%

commit v1 on v0

v1 whole, which is shorter than its diff:
```python
import functools
import math

import jax
import jax.numpy as jnp
from jax import lax
from jax.experimental import pallas as pl
from jax.experimental.pallas import tpu as pltpu
from jax.sharding import Mesh
from jax.sharding import PartitionSpec as P

MESH = pl.DeviceIdType.MESH
NAMES = ("pipe", "y", "zh", "x", "c")
SECTIONS, YS, ZHS, XS, CORES = 8, 8, 2, 4, 2
EXPS = XS * CORES
ROWS, HALF, DH = 128, 64, 128
WIDTH, HEADS, KVH = 4096, 32, 2
KV = 2 * KVH * DH
PART = KV // CORES
NDOC = 8
REACH = 5
KEYS = REACH * ROWS
SHARD = 32
EPSILON = 1e-06
HIDDEN = -1e30
CHUNK = 4
LOG2E = 1.4426950408889634


def kernel(
    q_hbm, k_hbm, v_hbm, r_hbm, dl_ref, g_hbm, w_hbm, ctx_hbm, kv_hbm,
    fbuf, tbuf, wbuf, gbuf, qv, rv, cv, lo, bias, ov,
    send_sems, load_sems, out_sems, z_recv, f_recv, t_recv, wz_recv, wy_recv,
    wx_recv, lo_recv, g_recv, o_recv,
):
    pipe, y, zh = lax.axis_index("pipe"), lax.axis_index("y"), lax.axis_index("zh")
    x, c = lax.axis_index("x"), lax.axis_index("c")
    z = zh * SECTIONS + pipe

    def at_z(step):
        there = lax.rem(z + step, SECTIONS * ZHS)
        return {"pipe": lax.rem(there, SECTIONS), "zh": there // SECTIONS}

    def at_y(step):
        return {"y": lax.rem(y + step + YS, YS)}

    def at_x(step):
        return {"x": lax.rem(x + step, XS)}

    twin = {"c": 1 - c}
    partner = {"zh": 1 - zh}
    behind, far_behind = at_z(15), at_z(7)
    ahead, far_ahead = at_z(1), at_z(9)

    pending = []

    def when(cond, act):
        if cond is None:
            act()
        else:
            pl.when(cond)(act)

    def send(src, dst, recv, dev, cond=None):
        index = len(pending)

        def make():
            return pltpu.make_async_remote_copy(
                src_ref=src, dst_ref=dst, send_sem=send_sems.at[index],
                recv_sem=recv, device_id=dev, device_id_type=MESH,
            )

        when(cond, lambda: make().start())
        pending.append((cond, make))

    def arrive(dst, recv, cond=None):
        def act():
            pltpu.make_async_remote_copy(
                src_ref=dst, dst_ref=dst, send_sem=send_sems.at[0],
                recv_sem=recv, device_id=twin, device_id_type=MESH,
            ).wait_recv()

        when(cond, act)

    loads = [
        (k_hbm.at[:HALF], fbuf.at[0, zh, :, : KVH * DH]),
        (v_hbm.at[:HALF], fbuf.at[0, zh, :, KVH * DH :]),
        (k_hbm.at[HALF:], tbuf.at[0, 1 - zh, :, : KVH * DH]),
        (v_hbm.at[HALF:], tbuf.at[0, 1 - zh, :, KVH * DH :]),
        (q_hbm, qv),
        (r_hbm, rv),
    ]
    loads = [pltpu.make_async_copy(a, b, load_sems.at[i]) for i, (a, b) in enumerate(loads)]
    for load in loads:
        load.start()

    barrier = pltpu.get_barrier_semaphore()
    greeted = [partner, twin] + [at_y(k) for k in (1, -1, 3, -3)] + [at_x(k) for k in (1, 2, 3)]
    for place in (behind, far_behind, ahead, far_ahead):
        greeted += [{**place, "c": core} for core in range(CORES)]
    for dev in greeted:
        pl.semaphore_signal(barrier, inc=1, device_id=dev, device_id_type=MESH)
    spill = [(7, 6, 2), (7, 5, 3), (7, 4, 4), (6, 5, 4)]
    for a, b in ((7, 5), (5, 7)):
        @pl.when(y == a)
        def _():
            pl.semaphore_signal(barrier, inc=1, device_id={"y": b}, device_id_type=MESH)

    for d in range(1, REACH):
        @pl.when(y < d)
        def _():
            fbuf[d] = jnp.zeros(fbuf.shape[1:], fbuf.dtype)

    row = lax.broadcasted_iota(jnp.int32, (HALF, 1), 0)
    lane = lax.broadcasted_iota(jnp.int32, (1, KEYS), 1)
    shard = y * ZHS + zh
    for run in range(2):
        query_pos = row + (shard if run == 0 else 2 * YS * ZHS - 1 - shard) * HALF
        top = y if run == 0 else 2 * YS - 1 - y
        key_pos = top * ROWS + lax.rem(lane, ROWS) - ROWS * lax.div(lane, ROWS)
        bound, first = jnp.int32(0), jnp.zeros((HALF, 1), jnp.int32)
        for doc in range(NDOC):
            bound = bound + dl_ref[doc]
            first = jnp.where(query_pos >= bound, bound, first)
        seen = (key_pos >= first) & (key_pos <= query_pos)
        bias[run] = jnp.where(seen, 0.0, HIDDEN)

    extra = jnp.where((y == 7) | (y == 5), 1, 0)
    pl.semaphore_wait(barrier, len(greeted) + extra)

    e = x * CORES + c
    for core in range(CORES):
        for place in (behind, far_behind):
            send(w_hbm.at[:, pl.ds(core * PART, PART)], wbuf.at[y, zh, e], wz_recv.at[zh, c], {**place, "c": core})
    for load in loads[:4]:
        load.wait()
    send(fbuf.at[0, zh], fbuf.at[0, zh], z_recv.at[0], partner)
    send(tbuf.at[0, 1 - zh], tbuf.at[0, 1 - zh], z_recv.at[1], partner)

    def copies(at, shift, d, half):
        slot = d + shift
        if slot < REACH:
            @pl.when(y == at)
            def _():
                pltpu.make_async_copy(fbuf.at[d, half], tbuf.at[slot, half], t_recv.at[slot, half]).start()

    def first_from_own(half):
        for k in (1, 3):
            send(fbuf.at[0, half], fbuf.at[k, half], f_recv.at[k, half], at_y(k), y + k < YS)
        for src, dst, slot in spill:
            send(fbuf.at[0, half], tbuf.at[slot, half], t_recv.at[slot, half], {"y": dst}, y == src)
        copies(7, 1, 0, half)
        copies(6, 3, 0, half)

    def second_from_own(half):
        for k in (1, 3):
            send(tbuf.at[0, half], tbuf.at[k, half], t_recv.at[k, half], at_y(-k), y >= k)

    def first_on(d, half):
        arrive(fbuf.at[d, half], f_recv.at[d, half], y >= d)
        if d % 2 == 1:
            send(fbuf.at[d, half], fbuf.at[d + 1, half], f_recv.at[d + 1, half], at_y(1), (y >= d) & (y + 1 < YS))
        copies(7, 1, d, half)
        copies(6, 3, d, half)

    def second_on(d, half):
        arrive(tbuf.at[d, half], t_recv.at[d, half], y + d < YS)
        if d % 2 == 1:
            send(tbuf.at[d, half], tbuf.at[d + 1, half], t_recv.at[d + 1, half], at_y(-1), (y + d < YS) & (y > 0))

    def w_part(r, side):
        return wbuf.at[lax.rem(y + YS - r, YS), :, pl.ds(lax.rem(x + side, XS) * CORES, CORES)]

    def w_along_x(r):
        part = w_part(r, 0)
        for k in range(1, XS):
            send(part, part, wx_recv.at[r, XS - k], at_x(k))

    def w_start():
        for h in range(ZHS):
            for core in range(CORES):
                arrive(wbuf.at[y, h, x * CORES + core], wz_recv.at[h, core])
        part = w_part(0, 0)
        for k in (1, -1, 3, -3):
            send(part, part, wy_recv.at[k % YS], at_y(k))
        w_along_x(0)

    def w_on(r):
        part = w_part(r, 0)
        arrive(part, wy_recv.at[r])
        if r in (1, 3):
            send(part, part, wy_recv.at[r + 1], at_y(1))
        if r == 7:
            send(part, part, wy_recv.at[r - 1], at_y(-1))
        w_along_x(r)

    own, other = zh, 1 - zh
    first_from_own(own)
    second_from_own(other)
    send(g_hbm, gbuf, g_recv, behind)
    for d in (1, 3):
        first_on(d, own)
        second_on(d, other)
    w_start()
    arrive(fbuf.at[0, other], z_recv.at[0])
    first_from_own(other)
    arrive(tbuf.at[0, own], z_recv.at[1])
    second_from_own(own)
    for r in (1, 7, 3, 5):
        w_on(r)
    for d in (1, 3):
        first_on(d, other)
        second_on(d, own)
    for r in (2, 6, 4):
        w_on(r)
    for d in (2, 4):
        for half in range(2):
            first_on(d, half)
    for load in loads[4:]:
        load.wait()

    scale = LOG2E / math.sqrt(DH)
    last = pipe == SECTIONS - 1
    ones = jnp.ones((KEYS, DH), jnp.bfloat16)

    def attend(run, group):
        buf = fbuf if run == 0 else tbuf
        own_lo = lo.at[c]
        rows = pl.ds(run * HALF, HALF)
        keys = buf[:, :, :, pl.ds(group * DH, DH)].reshape(KEYS, DH)
        values = buf[:, :, :, pl.ds((KVH + group) * DH, DH)].reshape(KEYS, DH)
        values = jnp.concatenate([values, ones], axis=1)
        per_group = HEADS // KVH

        def step(j, carry):
            base = (group * per_group + j * CHUNK) * DH
            cols = [pl.ds(pl.multiple_of(base + i * DH, DH), DH) for i in range(CHUNK)]
            queries = jnp.concatenate([qv[rows, col] for col in cols], axis=0)
            scores = lax.dot_general(
                queries, keys, (((1,), (1,)), ((), ())), preferred_element_type=jnp.float32
            )
            scores = scores.reshape(CHUNK, HALF, KEYS) * scale + bias[run]
            weights = jnp.exp2(scores - jnp.max(scores, axis=2, keepdims=True))
            rounded = weights.astype(jnp.bfloat16).reshape(CHUNK * HALF, KEYS)
            mixed = jnp.dot(rounded, values, preferred_element_type=jnp.float32)
            mixed = (mixed[:, :DH] / mixed[:, DH:]).astype(jnp.bfloat16)
            for i, col in enumerate(cols):
                context = mixed[i * HALF : (i + 1) * HALF]
                cv[rows, col] = context
                out = (rv[rows, col].astype(jnp.float32) + context.astype(jnp.float32)).astype(jnp.bfloat16)
                out = jnp.where(last, jnp.zeros_like(out), out)
                own_lo[rows, col] = out
            return carry

        lax.fori_loop(0, per_group // CHUNK, step, 0)
        part = lo.at[c, rows, pl.ds(group * per_group * DH, per_group * DH)]
        send(part, part, lo_recv.at[run, group], twin)

    outs = [
        pltpu.make_async_copy(cv.at[pl.ds(run * HALF, HALF)], ctx_hbm.at[pl.ds(run * HALF, HALF)], out_sems.at[run])
        for run in range(2)
    ]
    attend(0, 0)
    attend(0, 1)
    outs[0].start()
    for d in (2, 4):
        for half in range(2):
            second_on(d, half)
    for d in range(1, REACH):
        for half in range(2):
            arrive(tbuf.at[d, half], t_recv.at[d, half], y + d >= YS)
    attend(1, 0)
    attend(1, 1)
    outs[1].start()
    arrive(gbuf, g_recv)
    for r in range(YS):
        for side in range(1, XS):
            arrive(w_part(r, side), wx_recv.at[r, side])
    for run in range(2):
        for group in range(KVH):
            part = lo.at[1 - c, pl.ds(run * HALF, HALF), pl.ds(group * (WIDTH // KVH), WIDTH // KVH)]
            arrive(part, lo_recv.at[run, group])

    tokens = CORES * ROWS
    squares = jnp.zeros((tokens, DH), jnp.float32)
    for i in range(WIDTH // DH):
        part = lo[:, :, pl.ds(i * DH, DH)].reshape(tokens, DH).astype(jnp.float32)
        squares = squares + part * part
    inverse = lax.rsqrt(jnp.sum(squares, axis=1, keepdims=True) / WIDTH + EPSILON)
    total = jnp.zeros((tokens, PART), jnp.float32)
    depth = WIDTH // YS
    for i in range(YS):
        cols = pl.ds(i * depth, depth)
        part = lo[:, :, cols].reshape(tokens, depth).astype(jnp.float32)
        normed = (part * inverse * gbuf[:, cols]).astype(jnp.bfloat16)
        total = total + jnp.dot(normed, wbuf[i].reshape(depth, PART), preferred_element_type=jnp.float32)
    ov[...] = total.astype(jnp.bfloat16).reshape(CORES, ROWS, PART)
    mine = kv_hbm.at[:, pl.ds(pl.multiple_of(c * PART, PART), PART)]
    for core in range(CORES):
        send(ov.at[core], mine, o_recv.at[c], {**ahead, "c": core})
    for out in outs:
        out.wait()
    for core in range(CORES):
        arrive(kv_hbm.at[:, pl.ds(core * PART, PART)], o_recv.at[core])
    for cond, make in pending:
        when(cond, lambda: make().wait_send())


def on_device(queries, key_rows, value_rows, residual, doc_lengths, norm_gain, kv_weight):
    bf16, f32 = jnp.bfloat16, jnp.float32
    anywhere = pl.BlockSpec(memory_space=pl.ANY)
    dma = pltpu.SemaphoreType.DMA
    context, kv_next = pl.pallas_call(
        kernel,
        out_shape=(
            jax.ShapeDtypeStruct((ROWS, WIDTH), bf16),
            jax.ShapeDtypeStruct((ROWS, KV), bf16),
        ),
        in_specs=[anywhere] * 4 + [pl.BlockSpec(memory_space=pltpu.SMEM)] + [anywhere] * 2,
        out_specs=(anywhere, anywhere),
        scratch_shapes=[
            pltpu.VMEM((REACH, ZHS, HALF, KV), bf16),
            pltpu.VMEM((REACH, ZHS, HALF, KV), bf16),
            pltpu.VMEM((YS, ZHS, EXPS, SHARD, PART), bf16),
            pltpu.VMEM((1, WIDTH), f32),
            pltpu.VMEM((ROWS, WIDTH), bf16),
            pltpu.VMEM((ROWS, WIDTH), bf16),
            pltpu.VMEM((ROWS, WIDTH), bf16),
            pltpu.VMEM((CORES, ROWS, WIDTH), bf16),
            pltpu.VMEM((2, HALF, KEYS), f32),
            pltpu.VMEM((CORES, ROWS, PART), bf16),
            dma((96,)),
            dma((6,)),
            dma((2,)),
            dma((2,)),
            dma((REACH, ZHS)),
            dma((REACH, ZHS)),
            dma((ZHS, CORES)),
            dma((YS,)),
            dma((YS, XS)),
            dma((2, KVH)),
            dma(()),
            dma((CORES,)),
        ],
        compiler_params=pltpu.CompilerParams(
            collective_id=0, has_side_effects=True, vmem_limit_bytes=60 * 2**20
        ),
    )(
        queries.reshape(ROWS, WIDTH),
        key_rows.reshape(ROWS, KVH * DH),
        value_rows.reshape(ROWS, KVH * DH),
        residual.reshape(ROWS, WIDTH),
        doc_lengths.reshape(NDOC),
        norm_gain,
        kv_weight.reshape(SHARD, KV),
    )
    return context.reshape(1, 1, ROWS, WIDTH), kv_next.reshape(1, 1, ROWS, KV)


def solution(mesh):
    finer = Mesh(mesh.devices.reshape(SECTIONS, YS, ZHS, XS, CORES), NAMES)
    tokens = P("pipe", ("x", "c"), ("y", "zh"), None)
    return jax.shard_map(
        on_device,
        mesh=finer,
        in_specs=(
            tokens, tokens, tokens, tokens,
            P("pipe", ("x", "c"), None),
            P("pipe", None),
            P("pipe", ("y", "zh", "x", "c"), None),
        ),
        out_specs=(tokens, tokens),
        check_vma=False,
    )
```

time: 293 us -> 73.4 us (0.25)
  waiting for transfers between devices: 220 us -> 0 us
  Pallas kernels: 0 us -> 69.5 us
  blocking collectives: 26.2 us -> 0 us
  between operations: 14.3 us -> 0.65 us
  local copies, waits for them, and re-layouts: 14.4 us -> 2.98 us
  matrix products: 9.89 us -> 0 us
  other arithmetic: 4.74 us -> 0 us
  starting transfers between devices: 3.3 us -> 0 us
    all_gather x2 -> x0, waiting for transfers between devices: 200 us -> none  [the longest x1 147 us: on_device(): full_weight = lax.all_gather(kv_weight, SEQ_EXP, axis=1, tiled=True)]
    pallas_call x0 -> x1, Pallas kernels: none -> 69.5 us  [on_device(): pl.pallas_call(kernel, out_shape=(jax.ShapeDtypeStruct((ROWS, WIDTH), bf1...]
    all_gather x1 -> x0, blocking collectives: 26.2 us -> none  [gather_axes(): shard = lax.all_gather(shard, axis, axis=dim, tiled=True)]
    ppermute x1 -> x0, waiting for transfers between devices: 18.6 us -> none  [shifted(): return lax.ppermute(block, axis, route)]
    dot_general x5 -> x0, matrix products: 9.89 us -> none  [the longest x1 3.6 us: on_device(): jnp.dot(normed, full_weight.reshape(row_width, kv_weight.shape[2]), prefe...]
    reduce_sum x4 -> x0, other arithmetic: 3.27 us -> none  [the longest x2 2.89 us: attend_run(): sums = jnp.sum(weights, axis=3, keepdims=True)]
    ppermute x1 -> x0, starting transfers between devices: 3.22 us -> none  [shifted(): return lax.ppermute(block, axis, route)]
    concatenate x4 -> x0, local copies, waits for them, and re-layouts: 2.99 us -> none  [the longest x3 2.82 us: to_natural(): return jnp.concatenate([first_half, second], axis=0)]
  transfers between devices with their start and end apart: 3 -> 0, of which waited for: 3 -> 0; matrix products, arithmetic and copies ran while one was open for 8% -> 0% of each run, Pallas kernels for 0% -> 0%
where the time goes in v1:
time: 73.4 us; the launch traced here: 73.2 us
  Pallas kernels  69.5 us (95%)
  local copies, waits for them, and re-layouts  2.98 us (4%)
    pallas_call x1, Pallas kernels, on_device(): pl.pallas_call(kernel, out_shape=(jax.ShapeDtypeStruct((ROWS, WIDTH), bf1...  69.5 us
    unnamed x4, local copies, waits for them, and re-layouts  2.98 us

profile of v1, /device:TPU:1, one launch (start us, length us, event | category | flops | bytes accessed | tf_op | source)
XLA Modules:
  0.0 73.2 jit_solution(4949720882553236685)
XLA Ops:
  0.6 69.5 %shard_map.86 = (bf16[128,4096]{1,0:T(8,128)(2,1)}, bf16[128,512]{1,0:T(8,128)(2,1)}) custom-call(bf16[128,4096]{1,0:T(8,128)(2,1)} %bitcast.8, bf16[128,256]{1,0:T(8,128)(2,1)} %bitcast.12, bf16[128,256]{1,0:T(8,128)(2,1)} %bitcast.13, bf16[128,4096]{1,0:T(8,128)(2,1)} %bitcast.9, s32[8]{0:T(128)} %bitcast.15, f32[1,4096]{1,0:T(1,128)} %g_hbm.1, ...), custom_call_target="tpu_custom_call" | custom-call | tf_op jit(solution)/shard_map/pallas_call | solution.py:312
  70.2 0.0 copy-start
  70.2 2.3 %copy.11 = bf16[1,1,128,4096]{3,2,1,0:T(8,128)(2,1)} copy(bf16[1,1,128,4096]{3,2,1,0:T(8,128)(2,1)} %bitcast.10) | data formatting | bytes 2097152
  72.5 0.0 copy-done
  72.5 0.7 copy.12
Async XLA Ops:
  70.2 2.3 %copy-start = (bf16[128,512]{1,0:T(8,128)(2,1)S(1)}, bf16[128,512]{1,0:T(8,128)(2,1)}, u32[]{:S(2)}) copy-start(bf16[128,512]{1,0:T(8,128)(2,1)} %get-tuple-element.5) | copy-start | bytes 393220

commit v2 on v1

--- a/solution.py
+++ b/solution.py
@@ -23,13 +23,13 @@
 SHARD = 32
 EPSILON = 1e-06
 HIDDEN = -1e30
-CHUNK = 4
+CHUNK = 16
 LOG2E = 1.4426950408889634
 
 
 def kernel(
-    q_hbm, k_hbm, v_hbm, r_hbm, dl_ref, g_hbm, w_hbm, ctx_hbm, kv_hbm,
-    fbuf, tbuf, wbuf, gbuf, qv, rv, cv, lo, bias, ov,
+    q_hbm, k_hbm, v_hbm, r_hbm, dl_hbm, g_hbm, w_hbm, ctx_hbm, kv_hbm,
+    fbuf, tbuf, wbuf, gbuf, qv, rv, cv, lo, bias, ov, keys_t, values_one, ss, dl_ref, wv,
     send_sems, load_sems, out_sems, z_recv, f_recv, t_recv, wz_recv, wy_recv,
     wx_recv, lo_recv, g_recv, o_recv,
 ):
@@ -80,18 +80,6 @@
             ).wait_recv()
 
         when(cond, act)
-
-    loads = [
-        (k_hbm.at[:HALF], fbuf.at[0, zh, :, : KVH * DH]),
-        (v_hbm.at[:HALF], fbuf.at[0, zh, :, KVH * DH :]),
-        (k_hbm.at[HALF:], tbuf.at[0, 1 - zh, :, : KVH * DH]),
-        (v_hbm.at[HALF:], tbuf.at[0, 1 - zh, :, KVH * DH :]),
-        (q_hbm, qv),
-        (r_hbm, rv),
-    ]
-    loads = [pltpu.make_async_copy(a, b, load_sems.at[i]) for i, (a, b) in enumerate(loads)]
-    for load in loads:
-        load.start()
 
     barrier = pltpu.get_barrier_semaphore()
     greeted = [partner, twin] + [at_y(k) for k in (1, -1, 3, -3)] + [at_x(k) for k in (1, 2, 3)]
@@ -105,11 +93,27 @@
         def _():
             pl.semaphore_signal(barrier, inc=1, device_id={"y": b}, device_id_type=MESH)
 
+    loads = [
+        (k_hbm.at[:HALF], fbuf.at[0, zh, :, : KVH * DH]),
+        (v_hbm.at[:HALF], fbuf.at[0, zh, :, KVH * DH :]),
+        (k_hbm.at[HALF:], tbuf.at[0, 1 - zh, :, : KVH * DH]),
+        (v_hbm.at[HALF:], tbuf.at[0, 1 - zh, :, KVH * DH :]),
+        (dl_hbm, dl_ref),
+        (w_hbm.at[:, :PART], wv.at[0]),
+        (w_hbm.at[:, PART:], wv.at[1]),
+        (q_hbm, qv),
+        (r_hbm, rv),
+    ]
+    loads = [pltpu.make_async_copy(a, b, load_sems.at[i]) for i, (a, b) in enumerate(loads)]
+    for load in loads:
+        load.start()
+
     for d in range(1, REACH):
         @pl.when(y < d)
         def _():
             fbuf[d] = jnp.zeros(fbuf.shape[1:], fbuf.dtype)
 
+    loads[4].wait()
     row = lax.broadcasted_iota(jnp.int32, (HALF, 1), 0)
     lane = lax.broadcasted_iota(jnp.int32, (1, KEYS), 1)
     shard = y * ZHS + zh
@@ -119,7 +123,7 @@
         key_pos = top * ROWS + lax.rem(lane, ROWS) - ROWS * lax.div(lane, ROWS)
         bound, first = jnp.int32(0), jnp.zeros((HALF, 1), jnp.int32)
         for doc in range(NDOC):
-            bound = bound + dl_ref[doc]
+            bound = bound + dl_ref[0, doc]
             first = jnp.where(query_pos >= bound, bound, first)
         seen = (key_pos >= first) & (key_pos <= query_pos)
         bias[run] = jnp.where(seen, 0.0, HIDDEN)
@@ -127,10 +131,11 @@
     extra = jnp.where((y == 7) | (y == 5), 1, 0)
     pl.semaphore_wait(barrier, len(greeted) + extra)
 
-    e = x * CORES + c
+    for load in loads[5:7]:
+        load.wait()
     for core in range(CORES):
         for place in (behind, far_behind):
-            send(w_hbm.at[:, pl.ds(core * PART, PART)], wbuf.at[y, zh, e], wz_recv.at[zh, c], {**place, "c": core})
+            send(wv.at[core], wbuf.at[y, x, zh, c], wz_recv.at[zh, c], {**place, "c": core})
     for load in loads[:4]:
         load.wait()
     send(fbuf.at[0, zh], fbuf.at[0, zh], z_recv.at[0], partner)
@@ -168,59 +173,78 @@
             send(tbuf.at[d, half], tbuf.at[d + 1, half], t_recv.at[d + 1, half], at_y(-1), (y + d < YS) & (y > 0))
 
     def w_part(r, side):
-        return wbuf.at[lax.rem(y + YS - r, YS), :, pl.ds(lax.rem(x + side, XS) * CORES, CORES)]
+        return wbuf.at[lax.rem(y + YS - r, YS), lax.rem(x + side, XS)]
 
     def w_along_x(r):
         part = w_part(r, 0)
         for k in range(1, XS):
             send(part, part, wx_recv.at[r, XS - k], at_x(k))
 
-    def w_start():
-        for h in range(ZHS):
-            for core in range(CORES):
-                arrive(wbuf.at[y, h, x * CORES + core], wz_recv.at[h, core])
-        part = w_part(0, 0)
+    def w_start(h):
+        for core in range(CORES):
+            arrive(wbuf.at[y, x, h, core], wz_recv.at[h, core])
+        part = w_part(0, 0).at[h]
         for k in (1, -1, 3, -3):
-            send(part, part, wy_recv.at[k % YS], at_y(k))
-        w_along_x(0)
-
-    def w_on(r):
-        part = w_part(r, 0)
-        arrive(part, wy_recv.at[r])
+            send(part, part, wy_recv.at[k % YS, h], at_y(k))
+
+    def w_on(r, h):
+        part = w_part(r, 0).at[h]
+        arrive(part, wy_recv.at[r, h])
         if r in (1, 3):
-            send(part, part, wy_recv.at[r + 1], at_y(1))
+            send(part, part, wy_recv.at[r + 1, h], at_y(1))
         if r == 7:
-            send(part, part, wy_recv.at[r - 1], at_y(-1))
-        w_along_x(r)
+            send(part, part, wy_recv.at[r - 1, h], at_y(-1))
 
     own, other = zh, 1 - zh
     first_from_own(own)
     second_from_own(other)
     send(g_hbm, gbuf, g_recv, behind)
+    ss[...] = jnp.zeros_like(ss)
+    near, far = ahead["zh"], 1 - ahead["zh"]
+    w_start(near)
     for d in (1, 3):
         first_on(d, own)
         second_on(d, other)
-    w_start()
+    w_start(far)
+    w_along_x(0)
+    for r in (1, 7, 3, 5):
+        w_on(r, near)
     arrive(fbuf.at[0, other], z_recv.at[0])
     first_from_own(other)
+    for r in (1, 7, 3, 5):
+        w_on(r, far)
+        w_along_x(r)
     arrive(tbuf.at[0, own], z_recv.at[1])
     second_from_own(own)
-    for r in (1, 7, 3, 5):
-        w_on(r)
     for d in (1, 3):
         first_on(d, other)
         second_on(d, own)
     for r in (2, 6, 4):
-        w_on(r)
+        w_on(r, near)
+        w_on(r, far)
+        w_along_x(r)
     for d in (2, 4):
         for half in range(2):
             first_on(d, half)
-    for load in loads[4:]:
+    for load in loads[7:]:
         load.wait()
 
     scale = LOG2E / math.sqrt(DH)
     last = pipe == SECTIONS - 1
     ones = jnp.ones((KEYS, DH), jnp.bfloat16)
+
+    def add_squares(core, run, group):
+        rows = pl.ds(run * HALF, HALF)
+        found = ss[core, rows]
+        for i in range(HEADS // KVH):
+            out = lo[core, rows, pl.ds((group * (HEADS // KVH) + i) * DH, DH)].astype(jnp.float32)
+            found = found + out * out
+        ss[core, rows] = found
+
+    def from_twin(run, group):
+        part = lo.at[1 - c, pl.ds(run * HALF, HALF), pl.ds(group * (WIDTH // KVH), WIDTH // KVH)]
+        arrive(part, lo_recv.at[run, group])
+        add_squares(1 - c, run, group)
 
     def attend(run, group):
         buf = fbuf if run == 0 else tbuf
@@ -228,20 +252,20 @@
         rows = pl.ds(run * HALF, HALF)
         keys = buf[:, :, :, pl.ds(group * DH, DH)].reshape(KEYS, DH)
         values = buf[:, :, :, pl.ds((KVH + group) * DH, DH)].reshape(KEYS, DH)
-        values = jnp.concatenate([values, ones], axis=1)
+        keys_t[...] = keys.T
+        values_one[:, :DH] = values
+        values_one[:, DH:] = ones
         per_group = HEADS // KVH
 
         def step(j, carry):
             base = (group * per_group + j * CHUNK) * DH
             cols = [pl.ds(pl.multiple_of(base + i * DH, DH), DH) for i in range(CHUNK)]
             queries = jnp.concatenate([qv[rows, col] for col in cols], axis=0)
-            scores = lax.dot_general(
-                queries, keys, (((1,), (1,)), ((), ())), preferred_element_type=jnp.float32
-            )
+            scores = jnp.dot(queries, keys_t[...], preferred_element_type=jnp.float32)
             scores = scores.reshape(CHUNK, HALF, KEYS) * scale + bias[run]
             weights = jnp.exp2(scores - jnp.max(scores, axis=2, keepdims=True))
             rounded = weights.astype(jnp.bfloat16).reshape(CHUNK * HALF, KEYS)
-            mixed = jnp.dot(rounded, values, preferred_element_type=jnp.float32)
+            mixed = jnp.dot(rounded, values_one[...], preferred_element_type=jnp.float32)
             mixed = (mixed[:, :DH] / mixed[:, DH:]).astype(jnp.bfloat16)
             for i, col in enumerate(cols):
                 context = mixed[i * HALF : (i + 1) * HALF]
@@ -254,6 +278,7 @@
         lax.fori_loop(0, per_group // CHUNK, step, 0)
         part = lo.at[c, rows, pl.ds(group * per_group * DH, per_group * DH)]
         send(part, part, lo_recv.at[run, group], twin)
+        add_squares(c, run, group)
 
     outs = [
         pltpu.make_async_copy(cv.at[pl.ds(run * HALF, HALF)], ctx_hbm.at[pl.ds(run * HALF, HALF)], out_sems.at[run])
@@ -269,30 +294,29 @@
         for half in range(2):
             arrive(tbuf.at[d, half], t_recv.at[d, half], y + d >= YS)
     attend(1, 0)
+    from_twin(0, 0)
+    from_twin(0, 1)
     attend(1, 1)
     outs[1].start()
+    from_twin(1, 0)
     arrive(gbuf, g_recv)
     for r in range(YS):
         for side in range(1, XS):
             arrive(w_part(r, side), wx_recv.at[r, side])
-    for run in range(2):
-        for group in range(KVH):
-            part = lo.at[1 - c, pl.ds(run * HALF, HALF), pl.ds(group * (WIDTH // KVH), WIDTH // KVH)]
-            arrive(part, lo_recv.at[run, group])
+    from_twin(1, 1)
 
     tokens = CORES * ROWS
-    squares = jnp.zeros((tokens, DH), jnp.float32)
-    for i in range(WIDTH // DH):
-        part = lo[:, :, pl.ds(i * DH, DH)].reshape(tokens, DH).astype(jnp.float32)
-        squares = squares + part * part
-    inverse = lax.rsqrt(jnp.sum(squares, axis=1, keepdims=True) / WIDTH + EPSILON)
+    squares = jnp.sum(ss[...].reshape(tokens, DH), axis=1, keepdims=True)
+    inverse = lax.rsqrt(squares / WIDTH + EPSILON)
     total = jnp.zeros((tokens, PART), jnp.float32)
     depth = WIDTH // YS
     for i in range(YS):
         cols = pl.ds(i * depth, depth)
         part = lo[:, :, cols].reshape(tokens, depth).astype(jnp.float32)
+        weights = [wbuf[i, j, h].reshape(CORES * SHARD, PART) for h in range(ZHS) for j in range(XS)]
+        weights = jnp.concatenate(weights, axis=0)
         normed = (part * inverse * gbuf[:, cols]).astype(jnp.bfloat16)
-        total = total + jnp.dot(normed, wbuf[i].reshape(depth, PART), preferred_element_type=jnp.float32)
+        total = total + jnp.dot(normed, weights, preferred_element_type=jnp.float32)
     ov[...] = total.astype(jnp.bfloat16).reshape(CORES, ROWS, PART)
     mine = kv_hbm.at[:, pl.ds(pl.multiple_of(c * PART, PART), PART)]
     for core in range(CORES):
@@ -315,12 +339,12 @@
             jax.ShapeDtypeStruct((ROWS, WIDTH), bf16),
             jax.ShapeDtypeStruct((ROWS, KV), bf16),
         ),
-        in_specs=[anywhere] * 4 + [pl.BlockSpec(memory_space=pltpu.SMEM)] + [anywhere] * 2,
+        in_specs=[anywhere] * 4 + [anywhere] + [anywhere] * 2,
         out_specs=(anywhere, anywhere),
         scratch_shapes=[
             pltpu.VMEM((REACH, ZHS, HALF, KV), bf16),
             pltpu.VMEM((REACH, ZHS, HALF, KV), bf16),
-            pltpu.VMEM((YS, ZHS, EXPS, SHARD, PART), bf16),
+            pltpu.VMEM((YS, XS, ZHS, CORES, SHARD, PART), bf16),
             pltpu.VMEM((1, WIDTH), f32),
             pltpu.VMEM((ROWS, WIDTH), bf16),
             pltpu.VMEM((ROWS, WIDTH), bf16),
@@ -328,14 +352,19 @@
             pltpu.VMEM((CORES, ROWS, WIDTH), bf16),
             pltpu.VMEM((2, HALF, KEYS), f32),
             pltpu.VMEM((CORES, ROWS, PART), bf16),
+            pltpu.VMEM((DH, KEYS), bf16),
+            pltpu.VMEM((KEYS, 2 * DH), bf16),
+            pltpu.VMEM((CORES, ROWS, DH), f32),
+            pltpu.SMEM((1, NDOC), jnp.int32),
+            pltpu.VMEM((CORES, SHARD, PART), bf16),
             dma((96,)),
-            dma((6,)),
+            dma((9,)),
             dma((2,)),
             dma((2,)),
             dma((REACH, ZHS)),
             dma((REACH, ZHS)),
             dma((ZHS, CORES)),
-            dma((YS,)),
+            dma((YS, ZHS)),
             dma((YS, XS)),
             dma((2, KVH)),
             dma(()),
@@ -349,7 +378,7 @@
         key_rows.reshape(ROWS, KVH * DH),
         value_rows.reshape(ROWS, KVH * DH),
         residual.reshape(ROWS, WIDTH),
-        doc_lengths.reshape(NDOC),
+        doc_lengths.reshape(1, NDOC),
         norm_gain,
         kv_weight.reshape(SHARD, KV),
     )

time: 73.4 us -> 71.7 us (0.977)
  Pallas kernels: 69.5 us -> 67.9 us
    pallas_call x1, Pallas kernels: 69.5 us -> 67.9 us  [on_device(): pl.pallas_call(kernel, out_shape=(jax.ShapeDtypeStruct((ROWS, WIDTH), bf1...]
where the time goes in v2:
time: 71.7 us; the launch traced here: 71.5 us
  Pallas kernels  67.9 us (95%)
  local copies, waits for them, and re-layouts  2.98 us (4%)
    pallas_call x1, Pallas kernels, on_device(): pl.pallas_call(kernel, out_shape=(jax.ShapeDtypeStruct((ROWS, WIDTH), bf1...  67.9 us
    unnamed x4, local copies, waits for them, and re-layouts  2.98 us

profile of v2, /device:TPU:1, one launch (start us, length us, event | category | flops | bytes accessed | tf_op | source)
XLA Modules:
  0.0 71.5 jit_solution(5521207842602184672)
XLA Ops:
  0.6 67.9 %shard_map.86 = (bf16[128,4096]{1,0:T(8,128)(2,1)}, bf16[128,512]{1,0:T(8,128)(2,1)}) custom-call(bf16[128,4096]{1,0:T(8,128)(2,1)} %bitcast.8, bf16[128,256]{1,0:T(8,128)(2,1)} %bitcast.12, bf16[128,256]{1,0:T(8,128)(2,1)} %bitcast.13, bf16[128,4096]{1,0:T(8,128)(2,1)} %bitcast.9, s32[1,8]{1,0:T(1,128)} %bitcast.15, f32[1,4096]{1,0:T(1,128)} %g_hbm.1, ...), custom_call_target="tpu_custom_call" | custom-call | tf_op jit(solution)/shard_map/pallas_call | solution.py:336
  68.5 0.0 copy-start
  68.5 2.3 %copy.11 = bf16[1,1,128,4096]{3,2,1,0:T(8,128)(2,1)} copy(bf16[1,1,128,4096]{3,2,1,0:T(8,128)(2,1)} %bitcast.10) | data formatting | bytes 2097152
  70.8 0.0 copy-done
  70.8 0.7 copy.12
Async XLA Ops:
  68.5 2.3 %copy-start = (bf16[128,512]{1,0:T(8,128)(2,1)S(1)}, bf16[128,512]{1,0:T(8,128)(2,1)}, u32[]{:S(2)}) copy-start(bf16[128,512]{1,0:T(8,128)(2,1)} %get-tuple-element.5) | copy-start | bytes 393220

commit v3 on v2

--- a/solution.py
+++ b/solution.py
@@ -298,33 +298,35 @@
     from_twin(0, 1)
     attend(1, 1)
     outs[1].start()
-    from_twin(1, 0)
     arrive(gbuf, g_recv)
     for r in range(YS):
         for side in range(1, XS):
             arrive(w_part(r, side), wx_recv.at[r, side])
-    from_twin(1, 1)
-
-    tokens = CORES * ROWS
-    squares = jnp.sum(ss[...].reshape(tokens, DH), axis=1, keepdims=True)
-    inverse = lax.rsqrt(squares / WIDTH + EPSILON)
-    total = jnp.zeros((tokens, PART), jnp.float32)
-    depth = WIDTH // YS
-    for i in range(YS):
-        cols = pl.ds(i * depth, depth)
-        part = lo[:, :, cols].reshape(tokens, depth).astype(jnp.float32)
-        weights = [wbuf[i, j, h].reshape(CORES * SHARD, PART) for h in range(ZHS) for j in range(XS)]
-        weights = jnp.concatenate(weights, axis=0)
-        normed = (part * inverse * gbuf[:, cols]).astype(jnp.bfloat16)
-        total = total + jnp.dot(normed, weights, preferred_element_type=jnp.float32)
-    ov[...] = total.astype(jnp.bfloat16).reshape(CORES, ROWS, PART)
-    mine = kv_hbm.at[:, pl.ds(pl.multiple_of(c * PART, PART), PART)]
-    for core in range(CORES):
-        send(ov.at[core], mine, o_recv.at[c], {**ahead, "c": core})
+    tokens, depth = CORES * HALF, WIDTH // YS
+    for run in range(2):
+        if run == 1:
+            from_twin(1, 0)
+            from_twin(1, 1)
+        rows = pl.ds(run * HALF, HALF)
+        squares = jnp.sum(ss[:, rows].reshape(tokens, DH), axis=1, keepdims=True)
+        inverse = lax.rsqrt(squares / WIDTH + EPSILON)
+        total = jnp.zeros((tokens, PART), jnp.float32)
+        for i in range(YS):
+            cols = pl.ds(i * depth, depth)
+            part = lo[:, rows, cols].reshape(tokens, depth).astype(jnp.float32)
+            weights = [wbuf[i, j, h].reshape(CORES * SHARD, PART) for h in range(ZHS) for j in range(XS)]
+            weights = jnp.concatenate(weights, axis=0)
+            normed = (part * inverse * gbuf[:, cols]).astype(jnp.bfloat16)
+            total = total + jnp.dot(normed, weights, preferred_element_type=jnp.float32)
+        ov[:, rows] = total.astype(jnp.bfloat16).reshape(CORES, HALF, PART)
+        mine = kv_hbm.at[rows, pl.ds(pl.multiple_of(c * PART, PART), PART)]
+        for core in range(CORES):
+            send(ov.at[core, rows], mine, o_recv.at[run, c], {**ahead, "c": core})
     for out in outs:
         out.wait()
-    for core in range(CORES):
-        arrive(kv_hbm.at[:, pl.ds(core * PART, PART)], o_recv.at[core])
+    for run in range(2):
+        for core in range(CORES):
+            arrive(kv_hbm.at[pl.ds(run * HALF, HALF), pl.ds(core * PART, PART)], o_recv.at[run, core])
     for cond, make in pending:
         when(cond, lambda: make().wait_send())
 
@@ -368,7 +370,7 @@
             dma((YS, XS)),
             dma((2, KVH)),
             dma(()),
-            dma((CORES,)),
+            dma((2, CORES)),
         ],
         compiler_params=pltpu.CompilerParams(
             collective_id=0, has_side_effects=True, vmem_limit_bytes=60 * 2**20

time: 71.7 us -> 70.5 us (0.983)
  Pallas kernels: 67.9 us -> 66.7 us
    pallas_call x1, Pallas kernels: 67.9 us -> 66.7 us  [on_device(): pl.pallas_call(kernel, out_shape=(jax.ShapeDtypeStruct((ROWS, WIDTH), bf1...]
where the time goes in v3:
time: 70.5 us; the launch traced here: 70.4 us
  Pallas kernels  66.7 us (95%)
  local copies, waits for them, and re-layouts  2.98 us (4%)
    pallas_call x1, Pallas kernels, on_device(): pl.pallas_call(kernel, out_shape=(jax.ShapeDtypeStruct((ROWS, WIDTH), bf1...  66.7 us
    unnamed x4, local copies, waits for them, and re-layouts  2.98 us

profile of v3, /device:TPU:1, one launch (start us, length us, event | category | flops | bytes accessed | tf_op | source)
XLA Modules:
  0.0 70.4 jit_solution(11050139325300319946)
XLA Ops:
  0.6 66.7 %shard_map.86 = (bf16[128,4096]{1,0:T(8,128)(2,1)}, bf16[128,512]{1,0:T(8,128)(2,1)}) custom-call(bf16[128,4096]{1,0:T(8,128)(2,1)} %bitcast.8, bf16[128,256]{1,0:T(8,128)(2,1)} %bitcast.12, bf16[128,256]{1,0:T(8,128)(2,1)} %bitcast.13, bf16[128,4096]{1,0:T(8,128)(2,1)} %bitcast.9, s32[1,8]{1,0:T(1,128)} %bitcast.15, f32[1,4096]{1,0:T(1,128)} %g_hbm.1, ...), custom_call_target="tpu_custom_call" | custom-call | tf_op jit(solution)/shard_map/pallas_call | solution.py:338
  67.4 0.0 copy-start
  67.4 2.3 %copy.11 = bf16[1,1,128,4096]{3,2,1,0:T(8,128)(2,1)} copy(bf16[1,1,128,4096]{3,2,1,0:T(8,128)(2,1)} %bitcast.10) | data formatting | bytes 2097152
  69.7 0.0 copy-done
  69.7 0.7 copy.12
Async XLA Ops:
  67.4 2.3 %copy-start = (bf16[128,512]{1,0:T(8,128)(2,1)S(1)}, bf16[128,512]{1,0:T(8,128)(2,1)}, u32[]{:S(2)}) copy-start(bf16[128,512]{1,0:T(8,128)(2,1)} %get-tuple-element.5) | copy-start | bytes 393220
